TPU v7x, 32 devices: a whole 2x2x4 slice. The times are simulated.
32 devices in a mesh: groups: 2 (over y), row: 4 (over x, core), col: 4 (over z).
Axes of the slice: x: 2, y: 2, z: 4, core: 2. Of those that a mesh axis runs over, the one named last changes fastest.
Arguments:
- adjacency: bfloat16 [8, 4, 32, 128, 128], P(('groups', 'row'), 'col'), parts along dimension 0, may hold values from 0.049804688 to 1
- tile_row: int32 [8, 4, 32], P(('groups', 'row'), 'col'), parts along dimension 0, may hold values from -1 to 7, as said below
- tile_col: int32 [8, 4, 32], P(('groups', 'row'), 'col'), parts along dimension 0, may hold values from -1 to 7, as said below
- seed_node: int32 [512], P('groups'), parts along dimension 0, may hold values from 0 to 4095
- teleport_block: int32 [512], P('groups'), parts along dimension 0, may hold values from 0 to 31
- previous: float32 [8192, 256], P(('groups', 'row', 'col')), parts along dimension 0, may hold values from 0.1 to 10
Outputs:
- rank_field: float32 [8192, 256], P(('groups', 'row', 'col')), parts along dimension 0
There are 2 independent parts, one for each index of `groups`. A program takes and returns all parts, laid end to end along the dimension named above; each array names one. Nothing has to cross between parts.
Inputs may be any that keep to these rules, and one draw needn't show every extreme that they name: On each device the slots with entries >= 0 come first, and tile_row and tile_col are -1 together on the other slots; a device's (tile_row, tile_col) pairs are distinct; in every part exactly one device has all 32 slots used and every other device uses between 5 and 10 of them. `tile_col`: empty exactly where tile_row is empty. In every part, for each index of row, at least one tile column holds no tile on any device with that index of row.
All inputs are finite; a program needn't handle non-finite values.
Results may differ from a plain program's by a relative error of at most 0.0003.
Values may be sent and summed in bfloat16 or wider, within the bound.
A program may use at most 64 MiB of HBM per device.

v0:
```python
import jax
import jax.numpy as jnp
from jax import lax
from jax.sharding import PartitionSpec as P

TILE = 128
ITERS = 3
damping = 0.85
highest = lax.Precision.HIGHEST


def teleport_weights(node_ids, seed_node, teleport_block):
    at_seed = (node_ids[:, None] == seed_node[None, :]).astype(jnp.float32)
    in_block = ((node_ids // TILE)[:, None] == teleport_block[None, :]).astype(jnp.float32)
    return 4.0 * at_seed + 2.0 * in_block


def block_sum(
    tile_stack, row_ids, col_ids, ordering, sorted_keys, rank_panel, first_row, block_rows
):
    slot_total = tile_stack.shape[0]
    tile_edge = tile_stack.shape[1]
    seed_width = rank_panel.shape[2]
    slot_batch = min(8, slot_total)
    first_live = jnp.sum((sorted_keys < first_row).astype(jnp.int32))
    past_live = jnp.sum((sorted_keys < first_row + block_rows).astype(jnp.int32))
    batches = (past_live - first_live + slot_batch - 1) // slot_batch

    def one_batch(batch_index, accumulated):
        for offset in range(slot_batch):
            position = first_live + batch_index * slot_batch + offset
            slot_index = lax.dynamic_index_in_dim(
                ordering, jnp.minimum(position, slot_total - 1), 0, keepdims=False
            )
            is_live = position < past_live
            target_row = lax.dynamic_index_in_dim(row_ids, slot_index, 0, keepdims=False)
            source_col = lax.dynamic_index_in_dim(col_ids, slot_index, 0, keepdims=False)
            target = jnp.clip(target_row - first_row, 0, block_rows - 1)
            source = jnp.maximum(source_col, 0)
            one_tile = lax.dynamic_index_in_dim(tile_stack, slot_index, 0, keepdims=False)
            panel_block = lax.dynamic_index_in_dim(rank_panel, source, 0, keepdims=False)
            product = jnp.dot(one_tile, panel_block, preferred_element_type=jnp.float32)
            current = lax.dynamic_index_in_dim(accumulated, target, 0, keepdims=False)
            updated = current + jnp.where(is_live, product, jnp.zeros_like(product))
            accumulated = lax.dynamic_update_index_in_dim(accumulated, updated, target, 0)
        return accumulated

    start_sum = jnp.zeros((block_rows, tile_edge, seed_width), jnp.float32)
    result = lax.fori_loop(0, batches, one_batch, start_sum)
    return result.reshape(block_rows * tile_edge, seed_width)


def on_device(adjacency, tile_row, tile_col, seed_node, teleport_block, previous):
    tile_stack = adjacency[0, 0]
    row_ids = tile_row[0, 0]
    col_ids = tile_col[0, 0]
    owned_rows, seed_width = previous.shape
    slot_total = tile_stack.shape[0]
    tile_edge = tile_stack.shape[1]
    row_devices = lax.axis_size("row")
    col_devices = lax.axis_size("col")
    tile_rows = owned_rows * row_devices // tile_edge
    tile_cols = owned_rows * col_devices // tile_edge
    sort_keys = jnp.where(row_ids >= 0, row_ids, tile_rows)
    slot_order = jnp.arange(slot_total, dtype=jnp.int32)
    sorted_keys, ordering = lax.sort((sort_keys, slot_order), num_keys=1, is_stable=True)
    col_place = (col_ids[:, None] == jnp.arange(tile_cols, dtype=jnp.int32)[None, :]).astype(
        jnp.float32
    )
    tile_sums = jnp.sum(tile_stack.astype(jnp.float32), axis=1)
    col_sums = jnp.einsum("tj,tb->jb", col_place, tile_sums, precision=highest).reshape(
        tile_cols * tile_edge
    )
    full_divisor = jnp.maximum(lax.psum(col_sums, "col"), 1.0)
    first_node = (lax.axis_index("row") * col_devices + lax.axis_index("col")) * owned_rows
    node_ids = first_node + jnp.arange(owned_rows, dtype=jnp.int32)
    teleport = teleport_weights(node_ids, seed_node, teleport_block)
    rank_field = previous
    for iteration in range(ITERS):
        gathered = lax.all_gather(rank_field, "col", axis=0, tiled=True)
        rank_panel = (gathered / full_divisor[:, None]).astype(jnp.bfloat16)
        rank_panel = rank_panel.reshape(tile_cols, tile_edge, seed_width)
        partial_sum = block_sum(
            tile_stack, row_ids, col_ids, ordering, sorted_keys, rank_panel, 0, tile_rows
        )
        summed = lax.psum_scatter(partial_sum, "row", scatter_dimension=0, tiled=True)
        rank_field = damping * summed + (1.0 - damping) * teleport
    return rank_field


def solution(mesh):
    in_specs = (
        P(("groups", "row"), "col", None, None, None),
        P(("groups", "row"), "col", None),
        P(("groups", "row"), "col", None),
        P("groups"),
        P("groups"),
        P(("groups", "row", "col"), None),
    )
    out_specs = P(("groups", "row", "col"), None)
    return jax.shard_map(
        on_device, mesh=mesh, in_specs=in_specs, out_specs=out_specs, check_vma=False
    )
```

profile of v0, /device:TPU:0, one launch (start us, length us, event | category | flops | bytes accessed | tf_op | source)
XLA Modules:
  0.0 590.8 jit_solution(7642503846385073427)
XLA Ops:
  6.5 0.7 all-gather.4.cloned.1.call-update
  7.3 0.7 compare_select_fusion
  8.0 1.1 sort.15
  9.0 0.7 fusion.195
  11.1 1.4 convert_reduce_fusion
  12.5 0.3 convolution_bitcast_fusion
  12.7 13.6 %psum.7 = f32[1024]{0:T(1024)S(1)} all-reduce(f32[1024]{0:T(1024)S(1)} %convolution_bitcast_fusion), channel_id=1, replica_groups=mesh['groups'=2,'row'=4,'col'=4] {'col'}, use_global_device_ids=true, to_apply=%region_4.5 | all-reduce | flops 1024 | bytes 8192 | tf_op jit(solution)/shard_map/psum | solution.py:74
  26.4 13.3 %all-gather.4.cloned.1.call-done = f32[1024,256]{1,0:T(8,128)} async-done(((f32[256,256]{1,0:T(8,128)}), f32[1024,256]{1,0:T(8,128)}) %all-gather.4.cloned.1.call-update) | async-done | bytes 1048592 | tf_op jit(solution)/shard_map/all_gather | solution.py:80
  39.6 1.4 divide_convert_fusion.2
  41.2 33.7 %while.30 = (s32[]{:T(128)}, f32[8,128,256]{2,1,0:T(8,128)S(1)}, s32[]{:T(128)}, s32[]{:T(128)}, s32[32]{0:T(128)S(1)}, /*index=5*/s32[32]{0:T(128)S(1)}, s32[]{...) while((s32[]{:T(128)}, f32[8,128,256]{2,1,0:T(8,128)S(1)}, ...), condition=%wide.region_6.7_spmd, body=%wide.region_5.6_spmd.sunk | while | flops 67633232 | bytes 4982441 | solution.py:49
  41.9 0.7 fusion.300
  57.6 0.7 fusion.301
  60.3 0.2 fusion.302
  62.3 0.2 fusion.303
  64.5 0.2 fusion.304
  66.5 0.2 fusion.305
  70.5 0.2 fusion.307
  72.6 0.2 fusion.308
  74.7 0.2 fusion.309
  74.9 0.9 copy-done.1
  76.0 124.4 %reduce-scatter.4.cloned.1.call-done = f32[256,256]{1,0:T(8,128)} async-done(((f32[1024,256]{1,0:T(8,128)}), f32[256,256]{1,0:T(8,128)}) %reduce-scatter.4.cloned.1.call-update) | async-done | bytes 262160 | tf_op jit(solution)/shard_map/reduce_scatter | solution.py:86
  200.4 1.8 fusion.192
  202.2 28.1 %all-gather.6.cloned.1.call-done = f32[1024,256]{1,0:T(8,128)} async-done(((f32[256,256]{1,0:T(8,128)}), f32[1024,256]{1,0:T(8,128)}) %all-gather.6.cloned.1.call-update) | async-done | bytes 1048592 | tf_op jit(solution)/shard_map/all_gather | solution.py:80
  230.3 1.4 divide_convert_fusion.1
  231.8 33.8 %while.31 = (s32[]{:T(128)}, f32[8,128,256]{2,1,0:T(8,128)S(1)}, s32[]{:T(128)}, s32[]{:T(128)}, s32[32]{0:T(128)S(1)}, /*index=5*/s32[32]{0:T(128)S(1)}, s32[]{...) while((s32[]{:T(128)}, f32[8,128,256]{2,1,0:T(8,128)S(1)}, ...), condition=%wide.region_9.10_spmd, body=%wide.region_8.9_spmd.sunk | while | flops 67633232 | bytes 4982441 | solution.py:49
  232.5 0.7 fusion.326
  248.3 0.7 fusion.327
  251.0 0.2 fusion.328
  257.2 0.2 fusion.331
  261.2 0.2 fusion.333
  263.3 0.2 fusion.334
  265.5 0.2 fusion.335
  265.7 1.0 copy-done.2
  266.7 124.6 %reduce-scatter.6.cloned.1.call-done = f32[256,256]{1,0:T(8,128)} async-done(((f32[1024,256]{1,0:T(8,128)}), f32[256,256]{1,0:T(8,128)}) %reduce-scatter.6.cloned.1.call-update) | async-done | bytes 262160 | tf_op jit(solution)/shard_map/reduce_scatter | solution.py:86
  391.3 1.8 multiply_add_fusion.1
  393.2 28.0 %all-gather.8.cloned.1.call-done = f32[1024,256]{1,0:T(8,128)} async-done(((f32[256,256]{1,0:T(8,128)}), f32[1024,256]{1,0:T(8,128)}) %all-gather.8.cloned.1.call-update) | async-done | bytes 1048592 | tf_op jit(solution)/shard_map/all_gather | solution.py:80
  421.2 1.4 divide_convert_fusion
  422.7 33.8 %while.32 = (s32[]{:T(128)}, f32[8,128,256]{2,1,0:T(8,128)S(1)}, s32[]{:T(128)}, s32[]{:T(128)}, s32[32]{0:T(128)S(1)}, /*index=5*/s32[32]{0:T(128)S(1)}, s32[]{...) while((s32[]{:T(128)}, f32[8,128,256]{2,1,0:T(8,128)S(1)}, ...), condition=%wide.region_12.13_spmd, body=%wide.region_11.12_spmd.sunk | while | flops 67633232 | bytes 4982441 | solution.py:49
  423.5 0.7 fusion.352
  439.2 0.7 fusion.353
  441.9 0.2 fusion.354
  446.0 0.2 fusion.356
  448.1 0.2 fusion.357
  452.2 0.2 fusion.359
  456.4 0.2 fusion.361
  456.6 1.0 copy-done
  457.5 124.6 %reduce-scatter.8.cloned.1.call-done = f32[256,256]{1,0:T(8,128)} async-done(((f32[1024,256]{1,0:T(8,128)}), f32[256,256]{1,0:T(8,128)}) %reduce-scatter.8.cloned.1.call-update) | async-done | bytes 262160 | tf_op jit(solution)/shard_map/reduce_scatter | solution.py:86
  582.2 1.8 multiply_add_fusion
  (61 shorter events, 2.1 us)
Async XLA Ops:
  6.5 5.9 %copy-start.5 = (s32[1,1,32]{2,1,0:T(1,128)S(1)}, s32[1,1,32]{2,1,0:T(1,128)}, u32[]{:S(2)}) copy-start(s32[1,1,32]{2,1,0:T(1,128)} %param.14) | copy-start | bytes 388
  6.5 33.1 %all-gather.4.cloned.1.call-start = ((), (), s32[]{:S(2)}) async-start(), calls=%async_computation.3 | async-start | bytes 1310720 | tf_op jit(solution)/shard_map/all_gather | solution.py:80
  7.3 193.1 %reduce-scatter.4.cloned.1.call-start = ((), (), s32[]{:S(2)}) async-start(), calls=%async_computation.4 | async-start | bytes 1310720 | tf_op jit(solution)/shard_map/reduce_scatter | solution.py:86
  26.4 14.8 %copy-start.3 = (bf16[1,1,32,128,128]{4,3,2,1,0:T(8,128)(2,1)S(1)}, bf16[1,1,32,128,128]{4,3,2,1,0:T(8,128)(2,1)}, u32[]{:S(2)}) copy-start(bf16[1,1,32,128,128]{4,3,2,1,0:T(8,128)(2,1)} %param.12) | copy-start | bytes 3145732
  26.4 14.8 %copy-start.4 = (s32[1,1,32]{2,1,0:T(1,128)S(1)}, s32[1,1,32]{2,1,0:T(1,128)}, u32[]{:S(2)}) copy-start(s32[1,1,32]{2,1,0:T(1,128)} %param.13) | copy-start | bytes 388
  74.9 1.0 copy-start.1
  74.9 125.5 %copy-start.6 = (s32[256]{0:T(256)S(1)}, s32[256]{0:T(256)}, u32[]{:S(2)}) copy-start(s32[256]{0:T(256)} %param.16) | copy-start | bytes 3076
  74.9 125.4 %copy-start.7 = (s32[256]{0:T(256)S(1)}, s32[256]{0:T(256)}, u32[]{:S(2)}) copy-start(s32[256]{0:T(256)} %param.15) | copy-start | bytes 3076
  75.9 154.4 %all-gather.6.cloned.1.call-start = ((), (), s32[]{:S(2)}) async-start(), calls=%async_computation.5 | async-start | bytes 1310720 | tf_op jit(solution)/shard_map/all_gather | solution.py:80
  202.2 189.1 %reduce-scatter.6.cloned.1.call-start = ((), (), s32[]{:S(2)}) async-start(), calls=%async_computation.6 | async-start | bytes 1310720 | tf_op jit(solution)/shard_map/reduce_scatter | solution.py:86
  265.6 1.0 copy-start.2
  266.6 154.6 %all-gather.8.cloned.1.call-start = ((), (), s32[]{:S(2)}) async-start(), calls=%async_computation.7 | async-start | bytes 1310720 | tf_op jit(solution)/shard_map/all_gather | solution.py:80
  393.1 189.1 %reduce-scatter.8.cloned.1.call-start = ((), (), s32[]{:S(2)}) async-start(), calls=%async_computation.8 | async-start | bytes 1310720 | tf_op jit(solution)/shard_map/reduce_scatter | solution.py:86
  456.5 1.0 copy-start
Sparse Core Ops, SparseCore 0:
  8.9 30.6 all-gather.3
  76.0 124.3 reduce-scatter.3
  202.3 27.9 all-gather.5
  266.8 124.4 reduce-scatter.5
  393.2 27.9 all-gather.7
  457.7 124.4 reduce-scatter.7
where the time goes:
time: 596 us; the launch traced here: 591 us
  waiting for transfers between devices  444 us (74%)
  loops' own time  92.9 us (16%)
  between operations  14.9 us (2%)
  other arithmetic  13.6 us (2%)
  blocking collectives  13.6 us (2%)
  local copies, waits for them, and re-layouts  7.78 us (1%)
    reduce_scatter x3, waiting for transfers between devices, on_device(): lax.psum_scatter(partial_sum, 'row', scatter_dimension=0, tiled=True)  374 us
    another operation x3, loops' own time, block_sum(): result = lax.fori_loop(0, batches, one_batch, start_sum)  92.9 us
    all_gather x3, waiting for transfers between devices, on_device(): gathered = lax.all_gather(rank_field, 'col', axis=0, tiled=True)  69.4 us
    psum x1, blocking collectives, on_device(): full_divisor = jnp.maximum(lax.psum(col_sums, 'col'), 1.0)  13.6 us
  transfers between devices with their start and end apart: 6, of which 6 were waited for; matrix products, arithmetic and copies ran while one was open for 1% of the time, Pallas kernels for 0%

commit v1 on v0

--- a/solution.py
+++ b/solution.py
@@ -77,7 +77,14 @@
     teleport = teleport_weights(node_ids, seed_node, teleport_block)
     rank_field = previous
     for iteration in range(ITERS):
-        gathered = lax.all_gather(rank_field, "col", axis=0, tiled=True)
+        ring = [rank_field]
+        for hop in range(3):
+            ring.append(lax.ppermute(ring[-1], "col", [(dev, (dev + 1) % 4) for dev in range(4)]))
+        gathered = jnp.roll(
+            jnp.concatenate(ring[::-1], axis=0),
+            (lax.axis_index("col") + 1) * ring[0].shape[0],
+            axis=0,
+        )
         rank_panel = (gathered / full_divisor[:, None]).astype(jnp.bfloat16)
         rank_panel = rank_panel.reshape(tile_cols, tile_edge, seed_width)
         partial_sum = block_sum(

time: 596 us -> 574 us (0.963)
  waiting for transfers between devices: 444 us -> 420 us
  starting transfers between devices: 0.21 us -> 6.22 us
    all_gather x3 -> x0, waiting for transfers between devices: 69.4 us -> none  [on_device(): gathered = lax.all_gather(rank_field, 'col', axis=0, tiled=True)]
    ppermute x0 -> x9, waiting for transfers between devices: none -> 65.5 us  [on_device(): lax.ppermute(ring[-1], 'col', [(dev, (dev + 1) % 4) for dev in range(4)])]
    reduce_scatter x3, waiting for transfers between devices: 374 us -> 354 us  [on_device(): lax.psum_scatter(partial_sum, 'row', scatter_dimension=0, tiled=True)]
    ppermute x0 -> x9, starting transfers between devices: none -> 6.14 us  [on_device(): lax.ppermute(ring[-1], 'col', [(dev, (dev + 1) % 4) for dev in range(4)])]
  transfers between devices with their start and end apart: 6 -> 12, of which waited for: 6 -> 11; matrix products, arithmetic and copies ran while one was open for 1% -> 1% of each run, Pallas kernels for 0% -> 0%
where the time goes in v1:
time: 574 us; the launch traced here: 568 us
  waiting for transfers between devices  420 us (73%)
  loops' own time  92 us (16%)
  between operations  14.6 us (3%)
  blocking collectives  12.2 us (2%)
  other arithmetic  11.7 us (2%)
  local copies, waits for them, and re-layouts  7.67 us (1%)
  starting transfers between devices  6.22 us (1%)
    reduce_scatter x3, waiting for transfers between devices, on_device(): lax.psum_scatter(partial_sum, 'row', scatter_dimension=0, tiled=True)  354 us
    another operation x3, loops' own time, block_sum(): result = lax.fori_loop(0, batches, one_batch, start_sum)  92 us
    ppermute x9, waiting for transfers between devices, on_device(): lax.ppermute(ring[-1], 'col', [(dev, (dev + 1) % 4) for dev in range(4)])  65.5 us
    psum x1, blocking collectives, on_device(): full_divisor = jnp.maximum(lax.psum(col_sums, 'col'), 1.0)  12.2 us
  transfers between devices with their start and end apart: 12, of which 11 were waited for; matrix products, arithmetic and copies ran while one was open for 1% of the time, Pallas kernels for 0%

profile of v1, /device:TPU:0, one launch (start us, length us, event | category | flops | bytes accessed | tf_op | source)
XLA Modules:
  0.0 568.2 jit_solution(17143875374984331848)
XLA Ops:
  6.5 3.0 collective-permute-start
  9.6 0.7 compare_select_fusion
  10.2 1.1 sort.15
  11.3 6.9 %collective-permute-done = f32[256,256]{1,0:T(8,128)S(1)} collective-permute-done((f32[256,256]{1,0:T(8,128)}, f32[256,256]{1,0:T(8,128)S(1)}, u32[]{:S(2)}, u32[]{:S(2)}) %collective-permute-start) | collective-permute-done | bytes 262176 | tf_op jit(solution)/shard_map/ppermute | solution.py:82
  18.2 1.4 convert_reduce_fusion
  19.6 0.2 convolution_bitcast_fusion
  19.8 7.6 %collective-permute-done.1 = f32[256,256]{1,0:T(8,128)S(1)} collective-permute-done((f32[256,256]{1,0:T(8,128)S(1)}, f32[256,256]{1,0:T(8,128)S(1)}, u32[]{:S(2)}, u32[]{:S(2)}) %collective-permute-start.1) | collective-permute-done | bytes 262176 | tf_op jit(solution)/shard_map/ppermute | solution.py:82
  27.5 0.7 fusion.222
  29.4 12.2 %psum.7 = f32[1024]{0:T(1024)S(1)} all-reduce(f32[1024]{0:T(1024)S(1)} %convolution_bitcast_fusion), channel_id=1, replica_groups=mesh['groups'=2,'row'=4,'col'=4] {'col'}, use_global_device_ids=true, to_apply=%region_4.6 | all-reduce | flops 1024 | bytes 8192 | tf_op jit(solution)/shard_map/psum | solution.py:74
  41.7 1.3 fusion.216
  43.1 33.5 %while.30 = (s32[]{:T(128)}, f32[8,128,256]{2,1,0:T(8,128)S(1)}, s32[]{:T(128)}, s32[]{:T(128)}, s32[32]{0:T(128)S(1)}, /*index=5*/s32[32]{0:T(128)S(1)}, s32[]{...) while((s32[]{:T(128)}, f32[8,128,256]{2,1,0:T(8,128)S(1)}, ...), condition=%wide.region_6.8_spmd, body=%wide.region_5.7_spmd.sunk | while | flops 67633232 | bytes 4982441 | solution.py:49
  43.8 0.7 fusion.327
  59.4 0.7 fusion.328
  62.0 0.2 fusion.329
  64.0 0.2 fusion.330
  70.2 0.2 fusion.333
  74.3 0.2 fusion.335
  76.4 0.2 fusion.336
  76.6 0.9 copy-done.1
  77.6 117.4 %reduce-scatter.4.cloned.1.call-done = f32[256,256]{1,0:T(8,128)} async-done(((f32[1024,256]{1,0:T(8,128)}), f32[256,256]{1,0:T(8,128)}) %reduce-scatter.4.cloned.1.call-update) | async-done | bytes 262160 | tf_op jit(solution)/shard_map/reduce_scatter | solution.py:93
  195.0 1.1 fusion.219
  196.1 1.6 collective-permute-start.3
  197.7 8.3 %collective-permute-done.3 = f32[256,256]{1,0:T(8,128)S(1)} collective-permute-done((f32[256,256]{1,0:T(8,128)S(1)}, f32[256,256]{1,0:T(8,128)S(1)}, u32[]{:S(2)}, u32[]{:S(2)}) %collective-permute-start.3) | collective-permute-done | bytes 262176 | tf_op jit(solution)/shard_map/ppermute | solution.py:82
  206.0 9.0 %collective-permute-done.4 = f32[256,256]{1,0:T(8,128)S(1)} collective-permute-done((f32[256,256]{1,0:T(8,128)S(1)}, f32[256,256]{1,0:T(8,128)S(1)}, u32[]{:S(2)}, u32[]{:S(2)}) %collective-permute-start.4) | collective-permute-done | bytes 262176 | tf_op jit(solution)/shard_map/ppermute | solution.py:82
  215.0 8.2 %collective-permute-done.5 = f32[256,256]{1,0:T(8,128)S(1)} collective-permute-done((f32[256,256]{1,0:T(8,128)S(1)}, f32[256,256]{1,0:T(8,128)S(1)}, u32[]{:S(2)}, u32[]{:S(2)}) %collective-permute-start.5) | collective-permute-done | bytes 262176 | tf_op jit(solution)/shard_map/ppermute | solution.py:82
  223.2 1.3 fusion.217
  224.6 33.5 %while.31 = (s32[]{:T(128)}, f32[8,128,256]{2,1,0:T(8,128)S(1)}, s32[]{:T(128)}, s32[]{:T(128)}, s32[32]{0:T(128)S(1)}, /*index=5*/s32[32]{0:T(128)S(1)}, s32[]{...) while((s32[]{:T(128)}, f32[8,128,256]{2,1,0:T(8,128)S(1)}, ...), condition=%wide.region_9.11_spmd, body=%wide.region_8.10_spmd.sunk | while | flops 67633232 | bytes 4982441 | solution.py:49
  225.3 0.7 fusion.353
  240.9 0.7 fusion.354
  245.5 0.2 fusion.356
  255.8 0.2 fusion.361
  258.0 1.0 copy-done.2
  259.1 118.4 %reduce-scatter.6.cloned.1.call-done = f32[256,256]{1,0:T(8,128)} async-done(((f32[1024,256]{1,0:T(8,128)}), f32[256,256]{1,0:T(8,128)}) %reduce-scatter.6.cloned.1.call-update) | async-done | bytes 262160 | tf_op jit(solution)/shard_map/reduce_scatter | solution.py:93
  377.5 1.1 multiply_add_fusion.1
  378.6 1.5 collective-permute-start.6
  380.1 8.4 %collective-permute-done.6 = f32[256,256]{1,0:T(8,128)S(1)} collective-permute-done((f32[256,256]{1,0:T(8,128)S(1)}, f32[256,256]{1,0:T(8,128)S(1)}, u32[]{:S(2)}, u32[]{:S(2)}) %collective-permute-start.6) | collective-permute-done | bytes 262176 | tf_op jit(solution)/shard_map/ppermute | solution.py:82
  388.5 9.0 %collective-permute-done.7 = f32[256,256]{1,0:T(8,128)S(1)} collective-permute-done((f32[256,256]{1,0:T(8,128)S(1)}, f32[256,256]{1,0:T(8,128)S(1)}, u32[]{:S(2)}, u32[]{:S(2)}) %collective-permute-start.7) | collective-permute-done | bytes 262176 | tf_op jit(solution)/shard_map/ppermute | solution.py:82
  397.5 8.2 %collective-permute-done.8 = f32[256,256]{1,0:T(8,128)S(1)} collective-permute-done((f32[256,256]{1,0:T(8,128)S(1)}, f32[256,256]{1,0:T(8,128)S(1)}, u32[]{:S(2)}, u32[]{:S(2)}) %collective-permute-start.8) | collective-permute-done | bytes 262176 | tf_op jit(solution)/shard_map/ppermute | solution.py:82
  405.6 1.3 fusion.218
  407.0 33.5 %while.32 = (s32[]{:T(128)}, f32[8,128,256]{2,1,0:T(8,128)S(1)}, s32[]{:T(128)}, s32[]{:T(128)}, s32[32]{0:T(128)S(1)}, /*index=5*/s32[32]{0:T(128)S(1)}, s32[]{...) while((s32[]{:T(128)}, f32[8,128,256]{2,1,0:T(8,128)S(1)}, ...), condition=%wide.region_12.14_spmd, body=%wide.region_11.13_spmd.sunk | while | flops 67633232 | bytes 4982441 | solution.py:49
  407.7 0.7 fusion.379
  423.3 0.7 fusion.380
  425.9 0.2 fusion.381
  428.0 0.2 fusion.382
  434.2 0.2 fusion.385
  440.5 1.0 copy-done
  441.5 118.5 %reduce-scatter.8.cloned.1.call-done = f32[256,256]{1,0:T(8,128)} async-done(((f32[1024,256]{1,0:T(8,128)}), f32[256,256]{1,0:T(8,128)}) %reduce-scatter.8.cloned.1.call-update) | async-done | bytes 262160 | tf_op jit(solution)/shard_map/reduce_scatter | solution.py:93
  559.9 1.8 multiply_add_fusion
  (72 shorter events, 3.0 us)
Async XLA Ops:
  6.5 35.1 %copy-start.6 = (f32[256,256]{1,0:T(8,128)S(1)}, f32[256,256]{1,0:T(8,128)}, u32[]{:S(2)}) copy-start(f32[256,256]{1,0:T(8,128)} %param.19) | copy-start | bytes 786436
  6.5 13.1 %copy-start.5 = (s32[1,1,32]{2,1,0:T(1,128)S(1)}, s32[1,1,32]{2,1,0:T(1,128)}, u32[]{:S(2)}) copy-start(s32[1,1,32]{2,1,0:T(1,128)} %param.16) | copy-start | bytes 388
  6.5 188.5 %reduce-scatter.4.cloned.1.call-start = ((), (), s32[]{:S(2)}) async-start(), calls=%async_computation.3 | async-start | bytes 1310720 | tf_op jit(solution)/shard_map/reduce_scatter | solution.py:93
  6.5 11.6 %collective-permute-start = (f32[256,256]{1,0:T(8,128)}, f32[256,256]{1,0:T(8,128)S(1)}, u32[]{:S(2)}, u32[]{:S(2)}) collective-permute-start(f32[256,256]{1,0:T(8,128)} %param.19), channel_id=1, source_target_pairs={{0,1},{1,2},{2,3},{3,0},{4,5},{5,6},{6,7},{7,4},{8,9},{9,10},{10,1... | collective-permute-start | bytes 786440 | tf_op jit(solution)/shard_map/ppermute | solution.py:82
  18.2 9.3 %collective-permute-start.1 = (f32[256,256]{1,0:T(8,128)S(1)}, f32[256,256]{1,0:T(8,128)S(1)}, u32[]{:S(2)}, u32[]{:S(2)}) collective-permute-start(f32[256,256]{1,0:T(8,128)S(1)} %collective-permute-done), channel_id=1, source_target_pairs={{0,1},{1,2},{2,3},{3,0},{4,5},{5,6},{6,7},{7,4},{8,9},{9,10},{10,1... | collective-permute-start | bytes 786440 | tf_op jit(solution)/shard_map/ppermute | solution.py:82
  27.5 14.2 %collective-permute-start.2 = (f32[256,256]{1,0:T(8,128)S(1)}, f32[256,256]{1,0:T(8,128)S(1)}, u32[]{:S(2)}, u32[]{:S(2)}) collective-permute-start(f32[256,256]{1,0:T(8,128)S(1)} %collective-permute-done.1), channel_id=1, source_target_pairs={{0,1},{1,2},{2,3},{3,0},{4,5},{5,6},{6,7},{7,4},{8,9},{9,10},{10,1... | collective-permute-start | bytes 786440 | tf_op jit(solution)/shard_map/ppermute | solution.py:82
  41.6 1.4 copy-start.3
  41.6 1.4 copy-start.4
  76.5 1.0 copy-start.1
  76.6 118.5 %copy-start.7 = (s32[256]{0:T(256)S(1)}, s32[256]{0:T(256)}, u32[]{:S(2)}) copy-start(s32[256]{0:T(256)} %param.18) | copy-start | bytes 3076
  76.6 118.5 %copy-start.8 = (s32[256]{0:T(256)S(1)}, s32[256]{0:T(256)}, u32[]{:S(2)}) copy-start(s32[256]{0:T(256)} %param.17) | copy-start | bytes 3076
  77.5 300.0 %reduce-scatter.6.cloned.1.call-start = ((), (), s32[]{:S(2)}) async-start(), calls=%async_computation.4 | async-start | bytes 1310720 | tf_op jit(solution)/shard_map/reduce_scatter | solution.py:93
  196.1 9.9 %collective-permute-start.3 = (f32[256,256]{1,0:T(8,128)S(1)}, f32[256,256]{1,0:T(8,128)S(1)}, u32[]{:S(2)}, u32[]{:S(2)}) collective-permute-start(f32[256,256]{1,0:T(8,128)S(1)} %fusion.219), channel_id=1, source_target_pairs={{0,1},{1,2},{2,3},{3,0},{4,5},{5,6},{6,7},{7,4},{8,9},{9,10},{10,1... | collective-permute-start | bytes 786440 | tf_op jit(solution)/shard_map/ppermute | solution.py:82
  206.0 9.0 %collective-permute-start.4 = (f32[256,256]{1,0:T(8,128)S(1)}, f32[256,256]{1,0:T(8,128)S(1)}, u32[]{:S(2)}, u32[]{:S(2)}) collective-permute-start(f32[256,256]{1,0:T(8,128)S(1)} %collective-permute-done.3), channel_id=1, source_target_pairs={{0,1},{1,2},{2,3},{3,0},{4,5},{5,6},{6,7},{7,4},{8,9},{9,10},{10,1... | collective-permute-start | bytes 786440 | tf_op jit(solution)/shard_map/ppermute | solution.py:82
  215.0 8.2 %collective-permute-start.5 = (f32[256,256]{1,0:T(8,128)S(1)}, f32[256,256]{1,0:T(8,128)S(1)}, u32[]{:S(2)}, u32[]{:S(2)}) collective-permute-start(f32[256,256]{1,0:T(8,128)S(1)} %collective-permute-done.4), channel_id=1, source_target_pairs={{0,1},{1,2},{2,3},{3,0},{4,5},{5,6},{6,7},{7,4},{8,9},{9,10},{10,1... | collective-permute-start | bytes 786440 | tf_op jit(solution)/shard_map/ppermute | solution.py:82
  258.0 1.0 copy-start.2
  259.0 300.9 %reduce-scatter.8.cloned.1.call-start = ((), (), s32[]{:S(2)}) async-start(), calls=%async_computation.5 | async-start | bytes 1310720 | tf_op jit(solution)/shard_map/reduce_scatter | solution.py:93
  378.6 9.9 %collective-permute-start.6 = (f32[256,256]{1,0:T(8,128)S(1)}, f32[256,256]{1,0:T(8,128)S(1)}, u32[]{:S(2)}, u32[]{:S(2)}) collective-permute-start(f32[256,256]{1,0:T(8,128)S(1)} %multiply_add_fusion.1), channel_id=1, source_target_pairs={{0,1},{1,2},{2,3},{3,0},{4,5},{5,6},{6,7},{7,4},{8,9},{9,10},{10,1... | collective-permute-start | bytes 786440 | tf_op jit(solution)/shard_map/ppermute | solution.py:82
  388.5 9.0 %collective-permute-start.7 = (f32[256,256]{1,0:T(8,128)S(1)}, f32[256,256]{1,0:T(8,128)S(1)}, u32[]{:S(2)}, u32[]{:S(2)}) collective-permute-start(f32[256,256]{1,0:T(8,128)S(1)} %collective-permute-done.6), channel_id=1, source_target_pairs={{0,1},{1,2},{2,3},{3,0},{4,5},{5,6},{6,7},{7,4},{8,9},{9,10},{10,1... | collective-permute-start | bytes 786440 | tf_op jit(solution)/shard_map/ppermute | solution.py:82
  397.5 8.2 %collective-permute-start.8 = (f32[256,256]{1,0:T(8,128)S(1)}, f32[256,256]{1,0:T(8,128)S(1)}, u32[]{:S(2)}, u32[]{:S(2)}) collective-permute-start(f32[256,256]{1,0:T(8,128)S(1)} %collective-permute-done.7), channel_id=1, source_target_pairs={{0,1},{1,2},{2,3},{3,0},{4,5},{5,6},{6,7},{7,4},{8,9},{9,10},{10,1... | collective-permute-start | bytes 786440 | tf_op jit(solution)/shard_map/ppermute | solution.py:82
  440.5 1.0 copy-start
Sparse Core Ops, SparseCore 0:
  77.7 117.3 reduce-scatter.3
  259.1 118.3 reduce-scatter.5
  441.6 118.2 reduce-scatter.7
